TPU v7x, 32 devices: a whole 2x2x4 slice. The times are simulated.
32 devices in a mesh: dp: 8 (over z, y), head: 4 (over x, core).
Axes of the slice: x: 2, y: 2, z: 4, core: 2. Of those that a mesh axis runs over, the one named last changes fastest.
Arguments:
- hidden_in: bfloat16 [2048, 2048], P(('dp', 'head')), may hold values from -6 to 6
- norm_gain: bfloat16 [2048], replicated, may hold values from 0.25 to 1.75
- w_query: bfloat16 [2048, 2048], P(None, 'head'), may hold values from -0.125 to 0.125
- key_weight: bfloat16 [2048, 1024], P(None, 'head'), may hold values from -0.125 to 0.125
- w_value: bfloat16 [2048, 1024], P(None, 'head'), may hold values from -0.125 to 0.125
- query_gain: bfloat16 [128], replicated, may hold values from 0.796875 to 4
- key_gain: bfloat16 [128], replicated, may hold values from 0.25 to 1.75
- w_out: bfloat16 [2048, 2048], P('head'), may hold values from -0.125 to 0.125
- prefix_root_keys: bfloat16 [1024, 1024], P('dp', 'head'), may hold values from -210 to 210
- prefix_root_values: bfloat16 [1024, 1024], P('dp', 'head'), may hold values from -6 to 6
- mid_keys: bfloat16 [4096, 1024], P('dp', 'head'), may hold values from -210 to 210
- mid_values: bfloat16 [4096, 1024], P('dp', 'head'), may hold values from -6 to 6
- mid_lengths: int32 [16], replicated, may hold values from 1 to 256, 2048 in all
- leaf_keys: bfloat16 [4096, 1024], P('dp', 'head'), may hold values from -6 to 6
- leaf_values: bfloat16 [4096, 1024], P('dp', 'head'), may hold values from -6 to 6
- leaf_lengths: int32 [64], P('dp'), may hold values from 1 to 64, 2048 in all
- token_request: int32 [8, 256], P('dp'), may hold values from 0 to 7, never falling along the last dimension, each value on 1 to 64 neighbouring positions
- request_node: int32 [8, 8], P('dp'), may hold values from 0 to 15, as said below
Outputs:
- attn_update: bfloat16 [2048, 2048], P(('dp', 'head'))
- cache_keys: bfloat16 [2048, 1024], P('dp', 'head')
- cache_values: bfloat16 [2048, 1024], P('dp', 'head')
Inputs may be any that keep to these rules, and one draw needn't show every extreme that they name: `token_request`: in each row requests 0 to 7 all occur, in rising order, each on 1 to 64 consecutive tokens; some request has exactly 64. `request_node`: node v is held by dp index v // 2; the 8 requests of one row have parents on 8 different dp indices, one each.
All inputs are finite; a program needn't handle non-finite values. No bound on the sum of `leaf_lengths` on one device may be relied on, other than what follows from the above.
Results may differ from a plain program's by a relative error of at most 0.039.
Values may be sent and summed in bfloat16 or wider, within the bound.
A program may use at most 128 MiB of HBM per device.

v0:
```python
import math
import jax
import jax.numpy as jnp
from jax import lax
from jax.sharding import PartitionSpec as P

MID_DEV = 2
MID_LEN = 256
EPS = 1e-06
THETA = 1000000.0
MASKED = -1e30


def rms_rows(values, gain):
    power = jnp.mean(values * values, axis=-1, keepdims=True)
    return values * lax.rsqrt(power + EPS) * gain


def rotate(values, positions):
    width = values.shape[-1]
    half = width // 2
    exponent = jnp.arange(half).astype(jnp.float32) * (2.0 / width)
    freqs = jnp.power(THETA, -exponent)
    angles = positions.astype(jnp.float32)[:, None] * freqs[None, :]
    cosine = jnp.cos(angles)[:, None, :]
    sine = jnp.sin(angles)[:, None, :]
    first = values[..., :half]
    second = values[..., half:]
    return jnp.concatenate(
        [first * cosine - second * sine, second * cosine + first * sine], axis=-1
    )


def body(
    hidden_in,
    norm_gain,
    w_query,
    key_weight,
    w_value,
    query_gain,
    key_gain,
    w_out,
    prefix_root_keys,
    prefix_root_values,
    mid_keys,
    mid_values,
    mid_lengths,
    leaf_keys,
    leaf_values,
    leaf_lengths,
    token_request,
    request_node,
):
    head_dim = query_gain.shape[0]
    query_width = w_query.shape[1]
    key_width = key_weight.shape[1]
    kv_heads = key_width // head_dim
    query_group = query_width // key_width
    scale = 1.0 / math.sqrt(head_dim)
    dp_count = lax.axis_size("dp")
    normalized_input = rms_rows(
        hidden_in.astype(jnp.float32), norm_gain.astype(jnp.float32)
    ).astype(jnp.bfloat16)
    piece = lax.all_gather(normalized_input, "head", axis=0, tiled=True)
    mixed = jnp.concatenate(
        [
            jnp.dot(piece, w_query, preferred_element_type=jnp.float32),
            jnp.dot(piece, key_weight, preferred_element_type=jnp.float32),
            jnp.dot(piece, w_value, preferred_element_type=jnp.float32),
        ],
        axis=1,
    )
    height = mixed.shape[0]
    segment = token_request[0]
    branch_nodes = request_node[0]
    requests = branch_nodes.shape[0]
    request_ids = jnp.arange(requests, dtype=jnp.int32)
    token_ids = jnp.arange(height, dtype=jnp.int32)
    member = segment[None, :] == request_ids[:, None]
    counts = jnp.sum(member.astype(jnp.int32), axis=1)
    earlier = request_ids[None, :] < request_ids[:, None]
    starts = jnp.sum(jnp.where(earlier, counts[None, :], 0), axis=1)
    offset = token_ids - jnp.sum(jnp.where(member, starts[:, None], 0), axis=0)
    node_total = mid_lengths.shape[0]
    node_match = branch_nodes[:, None] == jnp.arange(node_total, dtype=jnp.int32)[None, :]
    branch_length = jnp.sum(jnp.where(node_match, mid_lengths[None, :], 0), axis=1)
    root_total = prefix_root_keys.shape[0] * dp_count
    positions = (
        root_total
        + jnp.sum(jnp.where(member, (branch_length + leaf_lengths)[:, None], 0), axis=0)
        + offset
    )
    query_part = mixed[:, :query_width].reshape(height, query_width // head_dim, head_dim)
    key_portion = mixed[:, query_width : query_width + key_width].reshape(
        height, kv_heads, head_dim
    )
    query_matrix = rotate(rms_rows(query_part, query_gain.astype(jnp.float32)), positions).astype(
        jnp.bfloat16
    )
    new_keys = rotate(rms_rows(key_portion, key_gain.astype(jnp.float32)), positions).astype(
        jnp.bfloat16
    )
    new_values = mixed[:, query_width + key_width :].astype(jnp.bfloat16)
    heads_query = query_matrix.reshape(height, kv_heads, query_group, head_dim)
    root_keys = lax.all_gather(prefix_root_keys, "dp", axis=0, tiled=True)
    root_values = lax.all_gather(prefix_root_values, "dp", axis=0, tiled=True)
    owner_of = branch_nodes // MID_DEV
    owner_ids = jnp.arange(dp_count, dtype=jnp.int32)
    owner_match = owner_of[None, :] == owner_ids[:, None]
    block_slot = jnp.sum(jnp.where(owner_match, (branch_nodes % MID_DEV)[None, :], 0), axis=1)
    block_request = jnp.sum(jnp.where(owner_match, request_ids[None, :], 0), axis=1)
    block_length = jnp.sum(jnp.where(owner_match, branch_length[None, :], 0), axis=1)
    wanted = lax.all_to_all(block_slot[:, None], "dp", split_axis=0, concat_axis=0, tiled=True)[
        :, 0
    ]
    second = (wanted == 1)[:, None, None]
    own_pairs = jnp.concatenate([mid_keys, mid_values], axis=1).reshape(
        MID_DEV, MID_LEN, 2 * key_width
    )
    sent = jnp.where(second, own_pairs[1][None], own_pairs[0][None])
    got = lax.all_to_all(sent, "dp", split_axis=0, concat_axis=0, tiled=True)
    got = got.reshape(dp_count * MID_LEN, 2 * key_width)
    leaf_each = leaf_keys.shape[0] // requests
    leaf_live = jnp.arange(leaf_each, dtype=jnp.int32)[None, :] < leaf_lengths[:, None]
    leaf_tag = jnp.where(leaf_live, request_ids[:, None], -1).reshape(-1)
    mid_live = jnp.arange(MID_LEN, dtype=jnp.int32)[None, :] < block_length[:, None]
    mid_tag = jnp.where(mid_live, block_request[:, None], -1).reshape(-1)
    own_mask = (segment[None, :] == segment[:, None]) & (token_ids[None, :] <= token_ids[:, None])
    mask = jnp.concatenate(
        [
            jnp.ones((height, root_keys.shape[0]), jnp.bool_),
            leaf_tag[None, :] == segment[:, None],
            own_mask,
            mid_tag[None, :] == segment[:, None],
        ],
        axis=1,
    )
    all_keys = jnp.concatenate(
        [root_keys, leaf_keys, new_keys.reshape(height, key_width), got[:, :key_width]], axis=0
    ).reshape(-1, kv_heads, head_dim)
    all_values = jnp.concatenate(
        [root_values, leaf_values, new_values, got[:, key_width:]], axis=0
    ).reshape(-1, kv_heads, head_dim)
    scores = jnp.einsum("tkgd,skd->kgts", heads_query, all_keys, preferred_element_type=jnp.float32)
    scores = jnp.where(mask[None, None], scores * scale, MASKED)
    weights = jnp.exp(scores - jnp.max(scores, axis=-1, keepdims=True))
    total = jnp.sum(weights, axis=-1)
    summed = jnp.einsum(
        "kgts,skd->kgtd",
        weights.astype(jnp.bfloat16),
        all_values,
        preferred_element_type=jnp.float32,
    )
    attn = (summed / total[..., None]).astype(jnp.bfloat16)
    attn = attn.transpose(2, 0, 1, 3).reshape(height, query_width)
    update = lax.psum_scatter(
        jnp.dot(attn, w_out, preferred_element_type=jnp.float32).astype(jnp.bfloat16),
        "head",
        scatter_dimension=0,
        tiled=True,
    )
    return (update, new_keys.reshape(height, key_width), new_values)


def solution(mesh):
    in_specs = (
        P(("dp", "head"), None),
        P(),
        P(None, "head"),
        P(None, "head"),
        P(None, "head"),
        P(),
        P(),
        P("head", None),
        P("dp", "head"),
        P("dp", "head"),
        P("dp", "head"),
        P("dp", "head"),
        P(),
        P("dp", "head"),
        P("dp", "head"),
        P("dp"),
        P("dp", None),
        P("dp", None),
    )
    out_specs = (P(("dp", "head"), None), P("dp", "head"), P("dp", "head"))
    return jax.shard_map(body, mesh=mesh, in_specs=in_specs, out_specs=out_specs, check_vma=False)
```

profile of v0, /device:TPU:0, one launch (start us, length us, event | category | flops | bytes accessed | tf_op | source)
XLA Modules:
  0.0 206.7 jit_solution(16049318135466380190)
XLA Ops:
  7.2 0.8 fusion.29
  8.0 0.9 select_reduce_fusion.6
  8.9 0.1 select_reduce_fusion.5
  9.0 0.7 copy.122
  9.7 7.3 %all-to-all-start = ((s32[8,1,1]{2,1,0:T(1,128)}), s32[8,1,1]{2,1,0:T(1,128)S(1)}, u32[]{:S(2)}, u32[]{:S(2)}) async-start(s32[8,1,1]{2,1,0:T(1,128)} %copy.122), calls=%async_computation | async-start | bytes 8192 | tf_op jit(solution)/shard_map/all_to_all | solution.py:113
  17.0 0.7 convert_element_type.58
  17.7 1.1 fusion.22
  18.8 1.8 fusion.24
  20.7 0.7 iota_select_fusion
  21.4 0.7 add.74
  22.1 1.0 constant_dynamic-update-slice_fusion.1
  23.0 1.0 constant_dynamic-update-slice_fusion
  24.0 0.8 fusion.35
  24.8 1.0 copy.133
  25.8 29.8 %all_gather.11 = bf16[1024,256]{0,1:T(8,128)(2,1)} all-gather(bf16[128,256]{0,1:T(8,128)(2,1)S(1)} %copy.133), channel_id=1, replica_groups=mesh['dp'=8,'head'=4] {'dp'}, dimensions={0}, use_global_device_ids=true | all-gather | bytes 589824 | tf_op jit(solution)/shard_map/all_gather | solution.py:106
  55.6 0.1 select_bitcast_fusion
  55.7 0.1 convert_reduce_fusion
  55.8 0.5 broadcast_compare_fusion
  56.2 0.1 select_n.68
  56.3 0.1 select_reduce_fusion.3
  56.4 0.1 copy.119
  56.5 27.1 %all_gather.9 = bf16[1024,256]{0,1:T(8,128)(2,1)S(1)} all-gather(bf16[128,256]{0,1:T(8,128)(2,1)S(1)} %copy.119), channel_id=1, replica_groups=mesh['dp'=8,'head'=4] {'dp'}, dimensions={0}, use_global_device_ids=true | all-gather | bytes 589824 | tf_op jit(solution)/shard_map/all_gather | solution.py:105
  83.6 0.1 select_reduce_fusion.1
  83.7 0.5 multiply_cosine_fusion
  84.2 0.1 broadcast_compare_fusion.1
  84.4 1.8 copy.124
  86.2 1.8 copy.123
  88.0 1.8 copy.134
  89.8 0.7 convert_element_type.65
  90.5 0.7 convert_element_type.60
  91.1 1.8 copy.120
  92.9 1.8 copy.127
  94.7 1.0 copy.126
  95.7 0.2 compare_reduce_fusion
  96.0 2.7 %broadcast_select_fusion = bf16[8,256,512]{1,2,0:T(8,128)(2,1)} fusion(pred[8]{0:T(512)(128)(4,1)S(1)} %compare_reduce_fusion, bf16[256,512]{0,1:T(8,128)(2,1)} %copy.124, bf16[256,512]{0,1:T(8,128)(2,1)} %copy.123), kind=kLoop, calls=%fused_computation.9 | loop fusion | flops 1048576 | bytes 2621448 | tf_op jit(solution)/shard_map/jit(_where)/select_n | solution.py:120
  98.6 4.4 %all-to-all-start.1 = ((bf16[8,256,512]{1,2,0:T(8,128)(2,1)}), bf16[8,256,512]{1,2,0:T(8,128)(2,1)}, u32[]{:S(2)}, u32[]{:S(2)}) async-start(bf16[8,256,512]{1,2,0:T(8,128)(2,1)} %broadcast_select_fusion), calls=%async_computation.1 | async-start | bytes 4194304 | tf_op jit(solution)/shard_map/all_to_all | solution.py:121
  103.1 0.1 fusion.28
  103.2 7.0 %pad_add_fusion = pred[256,3840]{0,1:T(8,128)(4,1)} fusion(pred[256,2048]{0,1:T(8,128)(4,1)S(1)} %broadcast_compare_fusion, pred[256,256]{0,1:T(8,128)(4,1)S(1)} %fusion.28, pred[256,512]{0,1:T(8,128)(4,1)S(1)} %broadcast_compare_fusion.1, pred[3840]{0:T(1024)(128)(4,1)S(1)} %pad.8.clone), kind=kLoop, calls=%fused_computation.7 | loop fusion | flops 2949120 | bytes 1707776 | tf_op jit(solution)/shard_map/concatenate | solution.py:129
  110.2 2.0 convolution_convert_fusion.1
  112.2 0.8 copy.135
  112.9 2.6 %fusion.36 = f32[256,512]{1,0:T(8,128)S(1)} fusion(bf16[256,2048]{1,0:T(8,128)(2,1)} %all-gather.2.cloned.1.call-done, bf16[2048,512]{1,0:T(8,128)(2,1)} %param.20), kind=kOutput, calls=%fused_computation.82 | convolution fusion | flops 536870912 | bytes 3670016 | tf_op jit(solution)/shard_map/dot_general | solution.py:67
  115.5 0.2 reshape.198
  115.7 0.3 multiply_reduce_fusion
  116.1 0.3 multiply_multiply_fusion
  116.5 0.5 subtract_convert_fusion
  117.0 0.8 copy.132
  117.8 0.7 copy.131
  118.5 0.5 multiply_reduce_fusion.1
  119.1 0.1 copy.121
  119.2 0.1 multiply_multiply_fusion.1
  119.3 0.2 multiply_subtract_fusion
  119.5 0.1 maximum_convert_fusion
  119.6 22.3 %all-to-all-done.1 = bf16[8,256,512]{1,2,0:T(8,128)(2,1)} async-done(((bf16[8,256,512]{1,2,0:T(8,128)(2,1)}), bf16[8,256,512]{1,2,0:T(8,128)(2,1)}, u32[]{:S(2)}, u32[]{:S(2)}) %all-to-all-start.1) | async-done | bytes 2097184 | tf_op jit(solution)/shard_map/all_to_all | solution.py:121
  141.9 1.9 copy.142
  143.8 1.1 fusion.34
  145.0 1.3 copy.128
  146.3 10.1 %fusion.2 = (f32[2,2,256]{2,1,0:T(2,128)S(1)}, f32[2,3840,256,2]{2,1,3,0:T(8,128)}) fusion(pred[256,3840]{0,1:T(8,128)(4,1)} %pad_add_fusion, bf16[256,2,2,64]{3,0,2,1:T(8,128)(2,1)} %bitcast.71, bf16[256,2,2,64]{3,0,2,1:T(8,128)(2,1)} %bitcast.72, bf16[2048,2,128]{2,0,1:T(8,128)(2,1)} %copy.128, bf16[256,2,128]{2,0,1:T(8,128)(2,1)S(1)} %maximum_convert_fusion, ...), kind=kOutput, calls=%fused_computation.4 | convolution fusion | flops 1026817024 | bytes 18944000 | tf_op jit(solution)/shard_map/tkgd,skd->kgts/dot_general | solution.py:144
  156.4 9.1 %fusion = f32[2,2,256]{2,1,0:T(2,128)S(1)} fusion(f32[2,3840,256,2]{2,1,3,0:T(8,128)} %get-tuple-element.41, f32[2,2,256]{2,1,0:T(2,128)S(1)} %get-tuple-element.40, pred[256,3840]{0,1:T(8,128)(4,1)} %pad_add_fusion), kind=kLoop, calls=%fused_computation.2 | loop fusion | flops 15727616 | bytes 16719872 | tf_op jit(solution)/shard_map/reduce_sum | solution.py:147
  165.5 1.2 pad_maximum_fusion
  166.8 7.7 %fusion.19 = bf16[256,2,2,128]{0,3,2,1:T(8,128)(2,1)S(1)} fusion(bf16[3840,2,128,1]{0,2,3,1:T(8,128)(2,1)S(1)} %bitcast.67, f32[2,3840,256,2]{2,1,3,0:T(8,128)} %get-tuple-element.41, f32[2,2,256]{2,1,0:T(2,128)S(1)} %get-tuple-element.40, pred[256,3840]{0,1:T(8,128)(4,1)S(1)} %copy-done.3, f32[256,2,2]{0,2,1:T(2,128)S(1)} %bitcast.80), kind=kOutput, calls=%fused_computation.22 | convolution fusion | flops 1022623744 | bytes 18948096 | tf_op jit(solution)/shard_map/kgts,skd->kgtd/dot_general | solution.py:148
  174.5 1.7 convolution_convert_fusion
  176.3 0.1 copy.137
  176.4 0.8 copy.138
  177.2 22.7 %reduce-scatter.2.cloned.1.call-done = bf16[64,2048]{1,0:T(8,128)(2,1)} async-done(((bf16[256,2048]{1,0:T(8,128)(2,1)}), bf16[64,2048]{1,0:T(8,128)(2,1)}) %reduce-scatter.2.cloned.1.call-update) | async-done | bytes 262160 | tf_op jit(solution)/shard_map/reduce_scatter | solution.py:156
  (40 shorter events, 0.3 us)
Async XLA Ops:
  7.2 167.4 %copy-start = (bf16[512,2048]{1,0:T(8,128)(2,1)S(1)}, bf16[512,2048]{1,0:T(8,128)(2,1)}, u32[]{:S(2)}) copy-start(bf16[512,2048]{1,0:T(8,128)(2,1)} %param.25) | copy-start | bytes 6291460
  7.2 48.5 %copy-start.12 = (s32[1,256]{1,0:T(1,128)S(1)}, s32[1,256]{1,0:T(1,128)}, u32[]{:S(2)}) copy-start(s32[1,256]{1,0:T(1,128)} %param.34) | copy-start | bytes 3076
  7.2 49.2 %copy-start.11 = (bf16[128,256]{1,0:T(8,128)(2,1)S(1)}, bf16[128,256]{1,0:T(8,128)(2,1)}, u32[]{:S(2)}) copy-start(bf16[128,256]{1,0:T(8,128)(2,1)} %param.26) | copy-start | bytes 196612
  9.7 86.0 %all-to-all-start = ((s32[8,1,1]{2,1,0:T(1,128)}), s32[8,1,1]{2,1,0:T(1,128)S(1)}, u32[]{:S(2)}, u32[]{:S(2)}) async-start(s32[8,1,1]{2,1,0:T(1,128)} %copy.122), calls=%async_computation | async-start | bytes 8192 | tf_op jit(solution)/shard_map/all_to_all | solution.py:113
  17.0 93.2 %all-gather.2.cloned.1.call-start = ((), (), s32[]{:S(2)}) async-start(), calls=%async_computation.3 | async-start | bytes 1310720 | tf_op jit(solution)/shard_map/all_gather | solution.py:64
  98.6 43.3 %all-to-all-start.1 = ((bf16[8,256,512]{1,2,0:T(8,128)(2,1)}), bf16[8,256,512]{1,2,0:T(8,128)(2,1)}, u32[]{:S(2)}, u32[]{:S(2)}) async-start(bf16[8,256,512]{1,2,0:T(8,128)(2,1)} %broadcast_select_fusion), calls=%async_computation.1 | async-start | bytes 4194304 | tf_op jit(solution)/shard_map/all_to_all | solution.py:121
  103.0 96.9 %reduce-scatter.2.cloned.1.call-start = ((), (), s32[]{:S(2)}) async-start(), calls=%async_computation.4 | async-start | bytes 1310720 | tf_op jit(solution)/shard_map/reduce_scatter | solution.py:156
  112.1 4.9 %copy-start.6 = (bf16[256,256]{1,0:T(8,128)(2,1)}, bf16[256,256]{1,0:T(8,128)(2,1)S(1)}, u32[]{:S(2)}) copy-start(bf16[256,256]{1,0:T(8,128)(2,1)S(1)} %convolution_convert_fusion.1) | copy-start | bytes 393220
  115.7 2.8 %copy-start.1 = (bf16[256,2048]{1,0:T(8,128)(2,1)S(1)}, bf16[256,2048]{1,0:T(8,128)(2,1)}, u32[]{:S(2)}) copy-start(bf16[256,2048]{1,0:T(8,128)(2,1)} %all-gather.2.cloned.1.call-done) | copy-start | bytes 3145732
  115.7 2.8 %copy-start.4 = (bf16[2048,256]{1,0:T(8,128)(2,1)S(1)}, bf16[2048,256]{1,0:T(8,128)(2,1)}, u32[]{:S(2)}) copy-start(bf16[2048,256]{1,0:T(8,128)(2,1)} %param.21) | copy-start | bytes 3145732
  119.6 26.7 %copy-start.8 = (bf16[256,2,128]{2,0,1:T(8,128)(2,1)}, bf16[256,2,128]{2,0,1:T(8,128)(2,1)S(1)}, u32[]{:S(2)}) copy-start(bf16[256,2,128]{2,0,1:T(8,128)(2,1)S(1)} %maximum_convert_fusion) | copy-start | bytes 393220
  143.8 2.5 %copy-start.10 = (bf16[512,2,128]{2,0,1:T(8,128)(2,1)S(1)}, bf16[512,2,128]{2,0,1:T(8,128)(2,1)}, u32[]{:S(2)}) copy-start(bf16[512,2,128]{2,0,1:T(8,128)(2,1)} %copy.127) | copy-start | bytes 786436
  156.3 9.1 %copy-start.2 = (bf16[2048,256]{0,1:T(8,128)(2,1)S(1)}, bf16[2048,256]{0,1:T(8,128)(2,1)}, u32[]{:S(2)}) copy-start(bf16[2048,256]{0,1:T(8,128)(2,1)} %get-tuple-element.27) | copy-start | bytes 3145732
  156.3 9.1 %copy-start.5 = (bf16[512,256]{0,1:T(8,128)(2,1)S(1)}, bf16[512,256]{0,1:T(8,128)(2,1)}, u32[]{:S(2)}) copy-start(bf16[512,256]{0,1:T(8,128)(2,1)} %copy.134) | copy-start | bytes 786436
  156.3 9.1 %copy-start.7 = (bf16[256,256]{0,1:T(8,128)(2,1)S(1)}, bf16[256,256]{0,1:T(8,128)(2,1)}, u32[]{:S(2)}) copy-start(bf16[256,256]{0,1:T(8,128)(2,1)} %copy.135) | copy-start | bytes 393220
  165.4 1.4 copy-start.3
  174.5 1.8 copy-start.9
Sparse Core Ops, SparseCore 0:
  20.8 18.0 all-gather.1
  176.4 23.4 reduce-scatter.1
where the time goes:
time: 208 us; the launch traced here: 207 us
  blocking collectives  56.8 us (27%)
  waiting for transfers between devices  45.1 us (22%)
  other arithmetic  31.6 us (15%)
  matrix products  24.6 us (12%)
  local copies, waits for them, and re-layouts  22.5 us (11%)
  between operations  14.4 us (7%)
  starting transfers between devices  11.7 us (6%)
    all_gather x1, blocking collectives, body(): root_values = lax.all_gather(prefix_root_values, 'dp', axis=0, tiled=True)  29.8 us
    all_gather x1, blocking collectives, body(): root_keys = lax.all_gather(prefix_root_keys, 'dp', axis=0, tiled=True)  27.1 us
    reduce_scatter x1, waiting for transfers between devices, body(): lax.psum_scatter(jnp.dot(attn, w_out, preferred_element_type=jnp.float32)...  22.7 us
    all_to_all x1, waiting for transfers between devices, body(): got = lax.all_to_all(sent, 'dp', split_axis=0, concat_axis=0, tiled=True)  22.3 us
    dot_general x1, matrix products, body(): jnp.einsum('tkgd,skd->kgts', heads_query, all_keys, preferred_element_typ...  10.1 us
    reduce_sum x1, other arithmetic, body(): total = jnp.sum(weights, axis=-1)  9.09 us
    dot_general x1, matrix products, body(): jnp.einsum('kgts,skd->kgtd', weights.astype(jnp.bfloat16), all_values, pr...  7.7 us
    all_to_all x1, starting transfers between devices, body(): lax.all_to_all(block_slot[:, None], 'dp', split_axis=0, concat_axis=0, ti...  7.28 us
  transfers between devices with their start and end apart: 4, of which 2 were waited for; matrix products, arithmetic and copies ran while one was open for 20% of the time, Pallas kernels for 0%

commit v1 on v0

--- a/solution.py
+++ b/solution.py
@@ -9,6 +9,27 @@
 EPS = 1e-06
 THETA = 1000000.0
 MASKED = -1e30
+
+
+def gather_around(x, axis, dim):
+    size, here, span = (lax.axis_size(axis), lax.axis_index(axis), x.shape[dim])
+    forward = [(i, (i + 1) % size) for i in range(size)]
+    backward = [(i, (i - 1) % size) for i in range(size)]
+    result = jnp.zeros((*x.shape[:dim], size * span, *x.shape[dim + 1 :]), x.dtype)
+    result = lax.dynamic_update_slice_in_dim(result, x, here * span, axis=dim)
+    from_left = from_right = x
+    halfway = size // 2
+    for step in range(1, halfway + 1):
+        from_left = lax.ppermute(from_left, axis, forward)
+        result = lax.dynamic_update_slice_in_dim(
+            result, from_left, (here - step) % size * span, axis=dim
+        )
+        if step < size - halfway:
+            from_right = lax.ppermute(from_right, axis, backward)
+            result = lax.dynamic_update_slice_in_dim(
+                result, from_right, (here + step) % size * span, axis=dim
+            )
+    return result
 
 
 def rms_rows(values, gain):
@@ -103,7 +124,7 @@
     new_values = mixed[:, query_width + key_width :].astype(jnp.bfloat16)
     heads_query = query_matrix.reshape(height, kv_heads, query_group, head_dim)
     root_keys = lax.all_gather(prefix_root_keys, "dp", axis=0, tiled=True)
-    root_values = lax.all_gather(prefix_root_values, "dp", axis=0, tiled=True)
+    root_values = gather_around(prefix_root_values, "dp", 0)
     owner_of = branch_nodes // MID_DEV
     owner_ids = jnp.arange(dp_count, dtype=jnp.int32)
     owner_match = owner_of[None, :] == owner_ids[:, None]

time: 208 us -> 215 us (1.034)
  blocking collectives: 56.8 us -> 28.7 us
  waiting for transfers between devices: 45.1 us -> 59.3 us
  starting transfers between devices: 11.7 us -> 23.2 us
  local copies, waits for them, and re-layouts: 22.5 us -> 29.3 us
    ppermute x0 -> x7, waiting for transfers between devices: none -> 32.1 us  [the longest x4 32.1 us: gather_around(): from_left = lax.ppermute(from_left, axis, forward)]
    all_gather x1 -> x0, blocking collectives: 29.8 us -> none  [body(): root_values = lax.all_gather(prefix_root_values, 'dp', axis=0, tiled=True)]
    all_to_all x1, waiting for transfers between devices: 22.3 us -> 0.01 us  [body(): got = lax.all_to_all(sent, 'dp', split_axis=0, concat_axis=0, tiled=True)]
    ppermute x0 -> x7, starting transfers between devices: none -> 15.5 us  [the longest x3 10.6 us: gather_around(): from_right = lax.ppermute(from_right, axis, backward)]
    dynamic_update_slice x0 -> x8, local copies, waits for them, and re-layouts: none -> 7.64 us  [the longest x4 3.39 us: gather_around(): lax.dynamic_update_slice_in_dim(result, from_left, (here - step) % size *...]
    reduce_scatter x1, waiting for transfers between devices: 22.7 us -> 27.2 us  [body(): lax.psum_scatter(jnp.dot(attn, w_out, preferred_element_type=jnp.float32)...]
    all_to_all x1, starting transfers between devices: 7.28 us -> 3.3 us  [body(): lax.all_to_all(block_slot[:, None], 'dp', split_axis=0, concat_axis=0, ti...]
    unnamed x33 -> x29, local copies, waits for them, and re-layouts: 6.52 us -> 6.49 us
  transfers between devices with their start and end apart: 4 -> 11, of which waited for: 2 -> 4; matrix products, arithmetic and copies ran while one was open for 20% -> 24% of each run, Pallas kernels for 0% -> 0%
where the time goes in v1:
time: 215 us; the launch traced here: 214 us
  waiting for transfers between devices  59.3 us (28%)
  other arithmetic  33.5 us (16%)
  local copies, waits for them, and re-layouts  29.3 us (14%)
  blocking collectives  28.7 us (13%)
  matrix products  25.5 us (12%)
  starting transfers between devices  23.2 us (11%)
  between operations  14.4 us (7%)
    ppermute x4, waiting for transfers between devices, gather_around(): from_left = lax.ppermute(from_left, axis, forward)  32.1 us
    all_gather x1, blocking collectives, body(): root_keys = lax.all_gather(prefix_root_keys, 'dp', axis=0, tiled=True)  28.7 us
    reduce_scatter x1, waiting for transfers between devices, body(): lax.psum_scatter(jnp.dot(attn, w_out, preferred_element_type=jnp.float32)...  27.2 us
    ppermute x3, starting transfers between devices, gather_around(): from_right = lax.ppermute(from_right, axis, backward)  10.6 us
    dot_general x1, matrix products, body(): jnp.einsum('tkgd,skd->kgts', heads_query, all_keys, preferred_element_typ...  10.2 us
    reduce_sum x1, other arithmetic, body(): total = jnp.sum(weights, axis=-1)  9.08 us
    dot_general x1, matrix products, body(): jnp.einsum('kgts,skd->kgtd', weights.astype(jnp.bfloat16), all_values, pr...  7.7 us
    unnamed x29, local copies, waits for them, and re-layouts  6.49 us
  transfers between devices with their start and end apart: 11, of which 4 were waited for; matrix products, arithmetic and copies ran while one was open for 24% of the time, Pallas kernels for 0%

profile of v1, /device:TPU:0, one launch (start us, length us, event | category | flops | bytes accessed | tf_op | source)
XLA Modules:
  0.0 213.8 jit_solution(15094773405789218817)
XLA Ops:
  7.2 1.7 copy.150
  8.9 3.0 %collective-permute-start = (bf16[128,256]{0,1:T(8,128)(2,1)}, bf16[128,256]{0,1:T(8,128)(2,1)}, u32[]{:S(2)}, u32[]{:S(2)}) collective-permute-start(bf16[128,256]{0,1:T(8,128)(2,1)} %copy.150), channel_id=1, source_target_pairs={{0,4},{4,8},{8,12},{12,16},{16,20},{20,24},{24,28},{28,0},{1,5},{5... | collective-permute-start | bytes 196616 | tf_op jit(solution)/shard_map/ppermute | solution.py:23
  11.9 3.0 %collective-permute-start.1 = (bf16[128,256]{0,1:T(8,128)(2,1)}, bf16[128,256]{0,1:T(8,128)(2,1)}, u32[]{:S(2)}, u32[]{:S(2)}) collective-permute-start(bf16[128,256]{0,1:T(8,128)(2,1)} %copy.150), channel_id=1, source_target_pairs={{0,28},{4,0},{8,4},{12,8},{16,12},{20,16},{24,20},{28,24},{1,29},{... | collective-permute-start | bytes 196616 | tf_op jit(solution)/shard_map/ppermute | solution.py:28
  14.9 0.7 fusion.29
  15.6 0.9 select_reduce_fusion.6
  16.6 0.7 copy.139
  17.3 3.3 %all-to-all-start = ((s32[8,1,1]{2,1,0:T(1,128)}), s32[8,1,1]{2,1,0:T(1,128)S(1)}, u32[]{:S(2)}, u32[]{:S(2)}) async-start(s32[8,1,1]{2,1,0:T(1,128)} %copy.139), calls=%async_computation | async-start | bytes 8192 | tf_op jit(solution)/shard_map/all_to_all | solution.py:134
  20.6 0.7 convert_element_type.58
  21.3 1.1 fusion.22
  22.4 1.8 fusion.24
  24.3 0.7 iota_select_fusion
  25.0 0.7 add.133
  25.6 1.5 fusion.28
  27.1 0.8 convert_reduce_fusion
  27.9 1.0 constant_dynamic-update-slice_fusion.1
  28.9 1.0 constant_dynamic-update-slice_fusion
  29.9 0.7 fusion.35
  30.7 1.1 broadcast_compare_fusion
  32.2 0.7 copy.136
  32.9 28.7 %all_gather.6 = bf16[1024,256]{0,1:T(8,128)(2,1)S(1)} all-gather(bf16[128,256]{0,1:T(8,128)(2,1)} %copy.136), channel_id=1, replica_groups=mesh['dp'=8,'head'=4] {'dp'}, dimensions={0}, use_global_device_ids=true | all-gather | bytes 589824 | tf_op jit(solution)/shard_map/all_gather | solution.py:126
  61.7 6.4 %pad_add_fusion = pred[256,3840]{0,1:T(8,128)(4,1)} fusion(pred[256,2048]{0,1:T(8,128)(4,1)S(1)} %broadcast_compare_fusion, pred[256,256]{0,1:T(8,128)(4,1)} %fusion.28, pred[256,512]{0,1:T(8,128)(4,1)S(1)} %broadcast_compare_fusion.1, pred[3840]{0:T(1024)(128)(4,1)S(1)} %pad.8.clone), kind=kLoop, calls=%fused_computation.7 | loop fusion | flops 2949120 | bytes 1707776 | tf_op jit(solution)/shard_map/concatenate | solution.py:150
  68.1 1.1 copy.141
  69.2 0.8 copy.140
  70.0 1.1 copy.153
  71.1 0.7 convert_element_type.65
  71.8 0.7 convert_element_type.60
  72.4 1.1 copy.137
  73.5 0.9 copy.144
  74.4 1.0 copy.143
  75.6 2.5 %broadcast_select_fusion = bf16[8,256,512]{1,2,0:T(8,128)(2,1)} fusion(pred[8]{0:T(512)(128)(4,1)S(1)} %compare_reduce_fusion, bf16[256,512]{0,1:T(8,128)(2,1)S(1)} %copy.141, bf16[256,512]{0,1:T(8,128)(2,1)} %copy.140), kind=kLoop, calls=%fused_computation.9 | loop fusion | flops 1048576 | bytes 2621448 | tf_op jit(solution)/shard_map/jit(_where)/select_n | solution.py:141
  78.1 4.3 %all-to-all-start.1 = ((bf16[8,256,512]{1,2,0:T(8,128)(2,1)}), bf16[8,256,512]{1,2,0:T(8,128)(2,1)}, u32[]{:S(2)}, u32[]{:S(2)}) async-start(bf16[8,256,512]{1,2,0:T(8,128)(2,1)} %broadcast_select_fusion), calls=%async_computation.1 | async-start | bytes 4194304 | tf_op jit(solution)/shard_map/all_to_all | solution.py:142
  82.5 0.5 multiply_cosine_fusion
  83.1 0.9 broadcast_in_dim.191
  83.9 1.5 constant_dynamic-update-slice_fusion.8
  85.4 1.9 collective-permute-start.2
  87.3 2.9 %collective-permute-start.3 = (bf16[128,256]{0,1:T(8,128)(2,1)}, bf16[128,256]{0,1:T(8,128)(2,1)S(1)}, u32[]{:S(2)}, u32[]{:S(2)}) collective-permute-start(bf16[128,256]{0,1:T(8,128)(2,1)} %collective-permute-done.1), channel_id=1, source_target_pairs={{0,28},{4,0},{8,4},{12,8},{16,12},{20,16},{24,20},{28,24},{1,29},{... | collective-permute-start | bytes 196616 | tf_op jit(solution)/shard_map/ppermute | solution.py:28
  90.1 1.5 constant_dynamic-update-slice_fusion.7
  91.6 1.5 constant_dynamic-update-slice_fusion.6
  93.1 25.4 %collective-permute-done.2 = bf16[128,256]{0,1:T(8,128)(2,1)S(1)} collective-permute-done((bf16[128,256]{0,1:T(8,128)(2,1)}, bf16[128,256]{0,1:T(8,128)(2,1)S(1)}, u32[]{:S(2)}, u32[]{:S(2)}) %collective-permute-start.2) | collective-permute-done | bytes 65568 | tf_op jit(solution)/shard_map/ppermute | solution.py:23
  118.5 4.7 %collective-permute-start.5 = (bf16[128,256]{0,1:T(8,128)(2,1)S(1)}, bf16[128,256]{0,1:T(8,128)(2,1)S(1)}, u32[]{:S(2)}, u32[]{:S(2)}) collective-permute-start(bf16[128,256]{0,1:T(8,128)(2,1)S(1)} %collective-permute-done.3), channel_id=1, source_target_pairs={{0,28},{4,0},{8,4},{12,8},{16,12},{20,16},{24,20},{28,24},{1,29},{... | collective-permute-start | bytes 196616 | tf_op jit(solution)/shard_map/ppermute | solution.py:28
  123.2 0.6 constant_dynamic-update-slice_fusion.5
  123.8 0.6 constant_dynamic-update-slice_fusion.4
  124.5 1.1 collective-permute-done.4
  125.5 0.6 constant_dynamic-update-slice_fusion.3
  126.2 0.7 constant_dynamic-update-slice_fusion.2
  126.8 5.7 %collective-permute-done.6 = bf16[128,256]{0,1:T(8,128)(2,1)S(1)} collective-permute-done((bf16[128,256]{0,1:T(8,128)(2,1)S(1)}, bf16[128,256]{0,1:T(8,128)(2,1)S(1)}, u32[]{:S(2)}, u32[]{:S(2)}) %collective-permute-start.6) | collective-permute-done | bytes 65568 | tf_op jit(solution)/shard_map/ppermute | solution.py:23
  132.5 0.6 constant_dynamic-update-slice_fusion.9
  133.1 2.0 convolution_convert_fusion.1
  135.1 0.8 copy.154
  135.9 3.4 %fusion.36 = f32[256,512]{1,0:T(8,128)} fusion(bf16[256,2048]{1,0:T(8,128)(2,1)} %all-gather.2.cloned.1.call-done, bf16[2048,512]{1,0:T(8,128)(2,1)} %param.20), kind=kOutput, calls=%fused_computation.90 | convolution fusion | flops 536870912 | bytes 3670016 | tf_op jit(solution)/shard_map/dot_general | solution.py:88
  139.3 1.2 reshape.198
  141.8 0.7 copy.149
  142.5 0.7 copy.148
  143.3 0.5 multiply_reduce_fusion.1
  144.4 1.9 copy.161
  146.3 1.1 fusion.34
  147.5 1.3 copy.145
  148.8 10.2 %fusion.2 = (f32[2,2,256]{2,1,0:T(2,128)S(1)}, f32[2,3840,256,2]{2,1,3,0:T(8,128)}) fusion(pred[256,3840]{0,1:T(8,128)(4,1)} %pad_add_fusion, bf16[256,2,2,64]{3,0,2,1:T(8,128)(2,1)} %bitcast.71, bf16[256,2,2,64]{3,0,2,1:T(8,128)(2,1)} %bitcast.72, bf16[2048,2,128]{2,0,1:T(8,128)(2,1)} %copy.145, bf16[256,2,128]{2,0,1:T(8,128)(2,1)S(1)} %maximum_convert_fusion, ...), kind=kOutput, calls=%fused_computation.4 | convolution fusion | flops 1026817024 | bytes 18944000 | tf_op jit(solution)/shard_map/tkgd,skd->kgts/dot_general | solution.py:165
  158.9 9.1 %fusion = f32[2,2,256]{2,1,0:T(2,128)S(1)} fusion(f32[2,3840,256,2]{2,1,3,0:T(8,128)} %get-tuple-element.41, f32[2,2,256]{2,1,0:T(2,128)S(1)} %get-tuple-element.40, pred[256,3840]{0,1:T(8,128)(4,1)} %pad_add_fusion), kind=kLoop, calls=%fused_computation.2 | loop fusion | flops 15727616 | bytes 16719872 | tf_op jit(solution)/shard_map/reduce_sum | solution.py:168
  168.1 1.3 pad_maximum_fusion
  169.4 7.7 %fusion.19 = bf16[256,2,2,128]{0,3,2,1:T(8,128)(2,1)S(1)} fusion(bf16[3840,2,128,1]{0,2,3,1:T(8,128)(2,1)S(1)} %bitcast.67, f32[2,3840,256,2]{2,1,3,0:T(8,128)} %get-tuple-element.41, f32[2,2,256]{2,1,0:T(2,128)S(1)} %get-tuple-element.40, pred[256,3840]{0,1:T(8,128)(4,1)S(1)} %copy-done.3, f32[256,2,2]{0,2,1:T(2,128)S(1)} %bitcast.80), kind=kOutput, calls=%fused_computation.22 | convolution fusion | flops 1022623744 | bytes 18948096 | tf_op jit(solution)/shard_map/kgts,skd->kgtd/dot_general | solution.py:169
  177.1 1.7 convolution_convert_fusion
  179.0 0.8 copy.157
  179.8 27.2 %reduce-scatter.2.cloned.1.call-done = bf16[64,2048]{1,0:T(8,128)(2,1)} async-done(((bf16[256,2048]{1,0:T(8,128)(2,1)}), bf16[64,2048]{1,0:T(8,128)(2,1)}) %reduce-scatter.2.cloned.1.call-update) | async-done | bytes 262160 | tf_op jit(solution)/shard_map/reduce_scatter | solution.py:177
  (58 shorter events, 3.0 us)
Async XLA Ops:
  7.2 169.9 %copy-start = (bf16[512,2048]{1,0:T(8,128)(2,1)S(1)}, bf16[512,2048]{1,0:T(8,128)(2,1)}, u32[]{:S(2)}) copy-start(bf16[512,2048]{1,0:T(8,128)(2,1)} %param.25) | copy-start | bytes 6291460
  7.2 24.7 %copy-start.10 = (s32[1,256]{1,0:T(1,128)S(1)}, s32[1,256]{1,0:T(1,128)}, u32[]{:S(2)}) copy-start(s32[1,256]{1,0:T(1,128)} %param.34) | copy-start | bytes 3076
  7.2 25.0 %copy-start.9 = (bf16[128,256]{1,0:T(8,128)(2,1)S(1)}, bf16[128,256]{1,0:T(8,128)(2,1)}, u32[]{:S(2)}) copy-start(bf16[128,256]{1,0:T(8,128)(2,1)} %param.26) | copy-start | bytes 196612
  8.9 76.5 %collective-permute-start = (bf16[128,256]{0,1:T(8,128)(2,1)}, bf16[128,256]{0,1:T(8,128)(2,1)}, u32[]{:S(2)}, u32[]{:S(2)}) collective-permute-start(bf16[128,256]{0,1:T(8,128)(2,1)} %copy.150), channel_id=1, source_target_pairs={{0,4},{4,8},{8,12},{12,16},{16,20},{20,24},{24,28},{28,0},{1,5},{5... | collective-permute-start | bytes 196616 | tf_op jit(solution)/shard_map/ppermute | solution.py:23
  11.9 75.4 %collective-permute-start.1 = (bf16[128,256]{0,1:T(8,128)(2,1)}, bf16[128,256]{0,1:T(8,128)(2,1)}, u32[]{:S(2)}, u32[]{:S(2)}) collective-permute-start(bf16[128,256]{0,1:T(8,128)(2,1)} %copy.150), channel_id=1, source_target_pairs={{0,28},{4,0},{8,4},{12,8},{16,12},{20,16},{24,20},{28,24},{1,29},{... | collective-permute-start | bytes 196616 | tf_op jit(solution)/shard_map/ppermute | solution.py:28
  17.3 58.1 %all-to-all-start = ((s32[8,1,1]{2,1,0:T(1,128)}), s32[8,1,1]{2,1,0:T(1,128)S(1)}, u32[]{:S(2)}, u32[]{:S(2)}) async-start(s32[8,1,1]{2,1,0:T(1,128)} %copy.139), calls=%async_computation | async-start | bytes 8192 | tf_op jit(solution)/shard_map/all_to_all | solution.py:134
  20.6 112.5 %all-gather.2.cloned.1.call-start = ((), (), s32[]{:S(2)}) async-start(), calls=%async_computation.3 | async-start | bytes 1310720 | tf_op jit(solution)/shard_map/all_gather | solution.py:85
  78.1 66.3 %all-to-all-start.1 = ((bf16[8,256,512]{1,2,0:T(8,128)(2,1)}), bf16[8,256,512]{1,2,0:T(8,128)(2,1)}, u32[]{:S(2)}, u32[]{:S(2)}) async-start(bf16[8,256,512]{1,2,0:T(8,128)(2,1)} %broadcast_select_fusion), calls=%async_computation.1 | async-start | bytes 4194304 | tf_op jit(solution)/shard_map/all_to_all | solution.py:142
  82.5 124.4 %reduce-scatter.2.cloned.1.call-start = ((), (), s32[]{:S(2)}) async-start(), calls=%async_computation.4 | async-start | bytes 1310720 | tf_op jit(solution)/shard_map/reduce_scatter | solution.py:177
  85.4 33.0 %collective-permute-start.2 = (bf16[128,256]{0,1:T(8,128)(2,1)}, bf16[128,256]{0,1:T(8,128)(2,1)S(1)}, u32[]{:S(2)}, u32[]{:S(2)}) collective-permute-start(bf16[128,256]{0,1:T(8,128)(2,1)} %collective-permute-done), channel_id=1, source_target_pairs={{0,4},{4,8},{8,12},{12,16},{16,20},{20,24},{24,28},{28,0},{1,5},{5... | collective-permute-start | bytes 196616 | tf_op jit(solution)/shard_map/ppermute | solution.py:23
  87.3 31.2 %collective-permute-start.3 = (bf16[128,256]{0,1:T(8,128)(2,1)}, bf16[128,256]{0,1:T(8,128)(2,1)S(1)}, u32[]{:S(2)}, u32[]{:S(2)}) collective-permute-start(bf16[128,256]{0,1:T(8,128)(2,1)} %collective-permute-done.1), channel_id=1, source_target_pairs={{0,28},{4,0},{8,4},{12,8},{16,12},{20,16},{24,20},{28,24},{1,29},{... | collective-permute-start | bytes 196616 | tf_op jit(solution)/shard_map/ppermute | solution.py:28
  118.5 7.1 %collective-permute-start.4 = (bf16[128,256]{0,1:T(8,128)(2,1)S(1)}, bf16[128,256]{0,1:T(8,128)(2,1)S(1)}, u32[]{:S(2)}, u32[]{:S(2)}) collective-permute-start(bf16[128,256]{0,1:T(8,128)(2,1)S(1)} %collective-permute-done.2), channel_id=1, source_target_pairs={{0,4},{4,8},{8,12},{12,16},{16,20},{20,24},{24,28},{28,0},{1,5},{5... | collective-permute-start | bytes 196616 | tf_op jit(solution)/shard_map/ppermute | solution.py:23
  118.5 7.7 %collective-permute-start.5 = (bf16[128,256]{0,1:T(8,128)(2,1)S(1)}, bf16[128,256]{0,1:T(8,128)(2,1)S(1)}, u32[]{:S(2)}, u32[]{:S(2)}) collective-permute-start(bf16[128,256]{0,1:T(8,128)(2,1)S(1)} %collective-permute-done.3), channel_id=1, source_target_pairs={{0,28},{4,0},{8,4},{12,8},{16,12},{20,16},{24,20},{28,24},{1,29},{... | collective-permute-start | bytes 196616 | tf_op jit(solution)/shard_map/ppermute | solution.py:28
  125.5 7.0 %collective-permute-start.6 = (bf16[128,256]{0,1:T(8,128)(2,1)S(1)}, bf16[128,256]{0,1:T(8,128)(2,1)S(1)}, u32[]{:S(2)}, u32[]{:S(2)}) collective-permute-start(bf16[128,256]{0,1:T(8,128)(2,1)S(1)} %collective-permute-done.4), channel_id=1, source_target_pairs={{0,4},{4,8},{8,12},{12,16},{16,20},{20,24},{24,28},{28,0},{1,5},{5... | collective-permute-start | bytes 196616 | tf_op jit(solution)/shard_map/ppermute | solution.py:23
  135.1 6.7 %copy-start.5 = (bf16[256,256]{1,0:T(8,128)(2,1)}, bf16[256,256]{1,0:T(8,128)(2,1)S(1)}, u32[]{:S(2)}) copy-start(bf16[256,256]{1,0:T(8,128)(2,1)S(1)} %convolution_convert_fusion.1) | copy-start | bytes 393220
  140.5 2.7 %copy-start.1 = (bf16[256,2048]{1,0:T(8,128)(2,1)S(1)}, bf16[256,2048]{1,0:T(8,128)(2,1)}, u32[]{:S(2)}) copy-start(bf16[256,2048]{1,0:T(8,128)(2,1)} %all-gather.2.cloned.1.call-done) | copy-start | bytes 3145732
  140.5 2.7 %copy-start.4 = (bf16[2048,256]{1,0:T(8,128)(2,1)S(1)}, bf16[2048,256]{1,0:T(8,128)(2,1)}, u32[]{:S(2)}) copy-start(bf16[2048,256]{1,0:T(8,128)(2,1)} %param.21) | copy-start | bytes 3145732
  144.4 4.4 %copy-start.7 = (bf16[256,2,128]{2,0,1:T(8,128)(2,1)}, bf16[256,2,128]{2,0,1:T(8,128)(2,1)S(1)}, u32[]{:S(2)}) copy-start(bf16[256,2,128]{2,0,1:T(8,128)(2,1)S(1)} %maximum_convert_fusion) | copy-start | bytes 393220
  158.9 9.1 %copy-start.2 = (bf16[2048,256]{0,1:T(8,128)(2,1)S(1)}, bf16[2048,256]{0,1:T(8,128)(2,1)}, u32[]{:S(2)}) copy-start(bf16[2048,256]{0,1:T(8,128)(2,1)} %get-tuple-element.27) | copy-start | bytes 3145732
  158.9 9.1 %copy-start.6 = (bf16[256,256]{0,1:T(8,128)(2,1)S(1)}, bf16[256,256]{0,1:T(8,128)(2,1)}, u32[]{:S(2)}) copy-start(bf16[256,256]{0,1:T(8,128)(2,1)} %copy.154) | copy-start | bytes 393220
  168.0 1.4 copy-start.3
  177.1 1.8 copy-start.8
Sparse Core Ops, SparseCore 0:
  24.4 18.1 all-gather.1
  179.0 27.8 reduce-scatter.1
